TPU v7x, 512 devices: a whole 4x4x16 slice. The times are simulated.
512 devices in a mesh: dp: 32 (over x, z_lo, core), seq: 16 (over z_hi, y).
Axes of the slice: x: 4, y: 4, z: 16 (z_hi: 4, z_lo: 4; z = z_hi * 4 + z_lo), core: 2. Of those that a mesh axis runs over, the one named last changes fastest.
Arguments:
- activations: bfloat16 [32, 2048, 1536], P('dp', 'seq'), may hold values from -6 to 6
- norm_gain: float32 [1536], replicated, may hold values from 0.25 to 1.75
- w_query: bfloat16 [1536, 1024], P('dp'), as said below
- w_key: bfloat16 [1536, 128], P('dp'), as said below
- w_value: bfloat16 [1536, 192], P('dp'), may hold values from -0.15625 to 0.15625
- w_out: bfloat16 [1536, 1536], P('dp'), may hold values from -0.15625 to 0.15625
- cotangent: bfloat16 [32, 2048, 1536], P('dp', 'seq'), may hold values from -6 to 6
Outputs:
- layer_out: bfloat16 [32, 2048, 1536], P('dp', 'seq')
- input_grad: bfloat16 [32, 2048, 1536], P('dp', 'seq')
- key_value_grad: float32 [1536, 320], P('dp')
Inputs may be any that keep to these rules, and one draw needn't show every extreme that they name: `w_query`: a projection matrix of full rank. `w_key`: a projection matrix of full rank.
All inputs are finite; a program needn't handle non-finite values.
Results may differ from a plain program's by a relative error of at most 0.034.
Values may be sent and summed in bfloat16 or wider, within the bound.
A program may use at most 64 MiB of HBM per device.

v0:
```python
import jax
import jax.numpy as jnp
from jax import lax
from jax.sharding import PartitionSpec as P

HEADS = 8
HQ = 128
DV = 192


epsilon = 1e-06


def per_device(activations, norm_gain, w_query, w_key, w_value, w_out, cotangent):
    acts_local = activations[0]
    grad_local = cotangent[0]
    query_full, key_full, value_full, outw_full = (
        lax.all_gather(w_query, "dp", axis=0, tiled=True),
        lax.all_gather(w_key, "dp", axis=0, tiled=True),
        lax.all_gather(w_value, "dp", axis=0, tiled=True),
        lax.all_gather(w_out, "dp", axis=0, tiled=True),
    )
    acts_wide = acts_local.astype(jnp.float32)
    rscale = lax.rsqrt(jnp.mean(acts_wide * acts_wide, axis=-1, keepdims=True) + epsilon)
    normed = (acts_wide * rscale * norm_gain).astype(jnp.bfloat16)
    qscale = HQ ** (-0.5)
    queries = (jnp.dot(normed, query_full, preferred_element_type=jnp.float32) * qscale).astype(
        jnp.bfloat16
    )
    keys_local = jnp.dot(normed, key_full, preferred_element_type=jnp.float32).astype(jnp.bfloat16)
    values_local = jnp.dot(normed, value_full, preferred_element_type=jnp.float32).astype(
        jnp.bfloat16
    )
    keys, values = (
        lax.all_gather(keys_local, "seq", axis=0, tiled=True),
        lax.all_gather(values_local, "seq", axis=0, tiled=True),
    )
    out_grad = jnp.dot(grad_local, outw_full.T, preferred_element_type=jnp.float32).astype(
        jnp.bfloat16
    )
    positions = acts_local.shape[0]
    total_rows = positions * HEADS
    block = min(512, total_rows)
    blocks = total_rows // block
    query_rows = queries.reshape(blocks, block, HQ)
    grad_rows = out_grad.reshape(blocks, block, DV)

    def block_pass(carry, pair):
        key_total, value_total = carry
        query_block, grad_block = pair
        scores = jnp.dot(query_block, keys.T, preferred_element_type=jnp.float32)
        top = jnp.max(scores, axis=-1, keepdims=True)
        expo = jnp.exp(scores - top)
        probs = expo / jnp.sum(expo, axis=-1, keepdims=True)
        probs_b = probs.astype(jnp.bfloat16)
        attended = jnp.dot(probs_b, values, preferred_element_type=jnp.float32).astype(jnp.bfloat16)
        dprob = jnp.dot(grad_block, values.T, preferred_element_type=jnp.float32)
        centre = jnp.sum(probs * dprob, axis=-1, keepdims=True)
        score_grad = (probs * (dprob - centre)).astype(jnp.bfloat16)
        query_grad = (
            jnp.dot(score_grad, keys, preferred_element_type=jnp.float32) * qscale
        ).astype(jnp.bfloat16)
        key_total = key_total + jnp.dot(
            score_grad.T, query_block, preferred_element_type=jnp.float32
        )
        value_total = value_total + jnp.dot(
            probs_b.T, grad_block, preferred_element_type=jnp.float32
        )
        return ((key_total, value_total), (attended, query_grad))

    start = (
        jnp.zeros((keys.shape[0], HQ), jnp.float32),
        jnp.zeros((keys.shape[0], DV), jnp.float32),
    )
    (key_terms, value_terms), (attended, query_grad) = lax.scan(
        block_pass, start, (query_rows, grad_rows)
    )
    attended = attended.reshape(positions, HEADS * DV)
    query_grad = query_grad.reshape(positions, HEADS * HQ)
    key_sum, value_sum = (
        lax.psum_scatter(
            key_terms.astype(jnp.bfloat16), "seq", scatter_dimension=0, tiled=True
        ).astype(jnp.float32),
        lax.psum_scatter(
            value_terms.astype(jnp.bfloat16), "seq", scatter_dimension=0, tiled=True
        ).astype(jnp.float32),
    )
    key_grad = key_sum.astype(jnp.bfloat16)
    value_grad = value_sum.astype(jnp.bfloat16)
    layer_out = (
        acts_wide + jnp.dot(attended, outw_full, preferred_element_type=jnp.float32)
    ).astype(jnp.bfloat16)
    normed_grad = jnp.dot(query_grad, query_full.T, preferred_element_type=jnp.float32)
    normed_grad = normed_grad + jnp.dot(key_grad, key_full.T, preferred_element_type=jnp.float32)
    normed_grad = normed_grad + jnp.dot(
        value_grad, value_full.T, preferred_element_type=jnp.float32
    )
    scaled = normed_grad * norm_gain
    inner = jnp.mean(scaled * acts_wide, axis=-1, keepdims=True)
    input_grad = (
        grad_local.astype(jnp.float32) + rscale * (scaled - acts_wide * rscale * rscale * inner)
    ).astype(jnp.bfloat16)
    weight_terms = jnp.concatenate(
        [
            jnp.dot(normed.T, key_grad, preferred_element_type=jnp.float32),
            jnp.dot(normed.T, value_grad, preferred_element_type=jnp.float32),
        ],
        axis=1,
    )
    row_share = lax.psum_scatter(
        weight_terms.astype(jnp.bfloat16), "dp", scatter_dimension=0, tiled=True
    )
    weight_grad = lax.psum(row_share, "seq").astype(jnp.float32)
    return (layer_out[None], input_grad[None], weight_grad)


def solution(mesh):
    in_specs = (
        P("dp", "seq", None),
        P(),
        P("dp", None),
        P("dp", None),
        P("dp", None),
        P("dp", None),
        P("dp", "seq", None),
    )
    out_specs = (P("dp", "seq", None), P("dp", "seq", None), P("dp", None))
    return jax.shard_map(
        per_device, mesh=mesh, in_specs=in_specs, out_specs=out_specs, check_vma=False
    )
```

profile of v0, /device:TPU:16, one launch (start us, length us, event | category | flops | bytes accessed | tf_op | source)
XLA Modules:
  0.0 732.9 jit_solution(15770494943124709025)
XLA Ops:
  7.2 0.0 copy-start.2
  7.2 0.0 all-gather.3.cloned.1.call-start
  7.2 0.7 all-gather.3.cloned.1.call-update
  7.9 0.0 all-gather.5.cloned.1.call-start
  8.0 0.7 all-gather.5.cloned.1.call-update
  8.7 0.0 reduce-scatter.8.cloned.1.call-start
  8.8 1.2 fusion.38
  9.9 50.2 %all_gather.22 = bf16[1536,192]{1,0:T(8,128)(2,1)S(1)} all-gather(bf16[48,192]{1,0:T(8,128)(2,1)} %param.13), channel_id=1, replica_groups=mesh['dp'=32,'seq'=16] {'dp'}, dimensions={0}, use_global_device_ids=true | all-gather | bytes 608256 | tf_op jit(solution)/shard_map/all_gather | solution.py:20
  60.2 1.4 convolution_convert_fusion.4
  61.6 61.0 %all_gather.23 = bf16[2048,192]{0,1:T(8,128)(2,1)S(1)} all-gather(bf16[128,192]{0,1:T(8,128)(2,1)S(1)} %convolution_convert_fusion.4), channel_id=1, replica_groups=mesh['dp'=32,'seq'=16] {'seq'}, dimensions={0}, use_global_device_ids=true | all-gather | bytes 835584 | tf_op jit(solution)/shard_map/all_gather | solution.py:36
  122.6 1.3 copy.15
  123.9 40.3 %all_gather.19 = bf16[1536,128]{1,0:T(8,128)(2,1)S(1)} all-gather(bf16[48,128]{1,0:T(8,128)(2,1)S(1)} %copy-done.11), channel_id=1, replica_groups=mesh['dp'=32,'seq'=16] {'dp'}, dimensions={0}, use_global_device_ids=true | all-gather | bytes 405504 | tf_op jit(solution)/shard_map/all_gather | solution.py:19
  164.2 0.3 convolution_convert_fusion.5
  164.5 51.5 %all_gather.20 = bf16[2048,128]{1,0:T(8,128)(2,1)S(1)} all-gather(bf16[128,128]{1,0:T(8,128)(2,1)S(1)} %convolution_convert_fusion.5), channel_id=1, replica_groups=mesh['dp'=32,'seq'=16] {'seq'}, dimensions={0}, use_global_device_ids=true | all-gather | bytes 557056 | tf_op jit(solution)/shard_map/all_gather | solution.py:35
  216.0 3.2 fusion.29
  219.2 1.1 reshape.36
  220.3 0.0 all-gather.5.cloned.1.call-done
  220.3 4.9 convolution_convert_fusion.3
  225.2 2.3 reshape.37
  227.4 31.5 %while.17 = (s32[]{:T(128)}, f32[2048,128]{1,0:T(8,128)S(1)}, f32[2048,192]{0,1:T(8,128)}, bf16[2,512,192]{1,2,0:T(8,128)(2,1)}, bf16[2,512,128]{2,1,0:T(8,128)(...) while((s32[]{:T(128)}, f32[2048,128]{1,0:T(8,128)S(1)}, ...), condition=%wide.region_5.6_spmd.clone, body=%wide.region_1.5_spmd.clone.sunk | while | flops 2033678848 | bytes 87387888 | solution.py:75
  227.4 0.8 fusion.94
  228.2 2.0 copy-done
  230.2 0.7 fusion.95
  231.0 4.6 convolution_add_fusion.7
  235.6 1.9 fusion.96
  237.4 1.5 multiply_reduce_fusion.2
  239.0 1.4 multiply_convert_fusion.2
  240.3 1.2 convolution_add_fusion.6
  241.5 1.4 fusion.97
  242.9 0.8 fusion.94
  243.7 2.0 copy-done
  245.7 0.7 fusion.95
  246.4 5.1 convolution_add_fusion.7
  251.6 1.9 fusion.96
  253.4 1.5 multiply_reduce_fusion.2
  255.0 1.4 multiply_convert_fusion.2
  256.3 1.2 convolution_add_fusion.6
  257.5 1.4 fusion.97
  258.9 0.8 convert_element_type.65
  259.7 0.0 reduce-scatter.8.cloned.1.call-update
  259.8 0.0 reduce-scatter.10.cloned.1.call-start
  259.8 1.5 convert_element_type.66
  261.3 1.3 copy.18
  262.6 0.0 reduce-scatter.10.cloned.1.call-update
  262.7 0.2 reduce-scatter.12.cloned.1.call-start
  262.9 1.8 reshape.39
  264.7 1.2 copy.16
  265.9 0.4 reshape.38
  266.3 102.4 %reduce-scatter.8.cloned.1.call-done = bf16[128,128]{1,0:T(8,128)(2,1)} async-done(((bf16[2048,128]{1,0:T(8,128)(2,1)}), bf16[128,128]{1,0:T(8,128)(2,1)}) %reduce-scatter.8.cloned.1.call-update) | async-done | bytes 32784 | tf_op jit(solution)/shard_map/reduce_scatter | solution.py:81
  368.7 1.1 convolution_convert_fusion.2
  369.8 112.0 %reduce-scatter.10.cloned.1.call-done = bf16[128,192]{1,0:T(8,128)(2,1)} async-done(((bf16[2048,192]{1,0:T(8,128)(2,1)}), bf16[128,192]{1,0:T(8,128)(2,1)}) %reduce-scatter.10.cloned.1.call-update) | async-done | bytes 49168
  481.7 1.2 convolution_convert_fusion.1
  483.0 0.1 pad_maximum_fusion
  483.1 1.4 copy.20
  484.5 0.0 reduce-scatter.12.cloned.1.call-update
  484.6 4.0 fusion.28
  488.6 0.3 fusion.48
  488.9 0.4 fusion.49
  489.3 1.3 fusion.39
  490.6 1.0 fusion.40
  491.7 139.7 %reduce-scatter.12.cloned.1.call-done = bf16[48,320]{1,0:T(8,128)(2,1)} async-done(((bf16[1536,320]{1,0:T(8,128)(2,1)}), bf16[48,320]{1,0:T(8,128)(2,1)}) %reduce-scatter.12.cloned.1.call-update) | async-done | bytes 30736
  631.4 0.9 copy.21
  632.3 93.3 %psum.7 = bf16[48,320]{0,1:T(8,128)(2,1)S(1)} all-reduce(bf16[48,320]{0,1:T(8,128)(2,1)S(1)} %copy.21), channel_id=1, replica_groups=mesh['dp'=32,'seq'=16] {'seq'}, use_global_device_ids=true, to_apply=%region_10.11 | all-reduce | flops 15360 | bytes 61440 | tf_op jit(solution)/shard_map/psum | solution.py:113
  725.6 0.7 copy.17
  (36 shorter events, 0.1 us)
Async XLA Ops:
  7.2 157.0 %copy-start.2 = (bf16[1,128,1536]{2,1,0:T(8,128)(2,1)S(1)}, bf16[1,128,1536]{2,1,0:T(8,128)(2,1)}, u32[]{:S(2)}) copy-start(bf16[1,128,1536]{2,1,0:T(8,128)(2,1)} %param.9) | copy-start | bytes 1179652
  7.2 157.0 %copy-start.9 = (f32[1536]{0:T(1024)S(1)}, f32[1536]{0:T(1024)}, u32[]{:S(2)}) copy-start(f32[1536]{0:T(1024)} %param.10) | copy-start | bytes 18436
  7.2 116.7 %copy-start.11 = (bf16[48,128]{1,0:T(8,128)(2,1)S(1)}, bf16[48,128]{1,0:T(8,128)(2,1)}, u32[]{:S(2)}) copy-start(bf16[48,128]{1,0:T(8,128)(2,1)} %param.12) | copy-start | bytes 36868
  7.2 208.8 %all-gather.3.cloned.1.call-start = ((), (), s32[]{:S(2)}) async-start(), calls=%async_computation.3 | async-start | bytes 3244032 | tf_op jit(solution)/shard_map/all_gather | solution.py:18
  7.9 212.4 %all-gather.5.cloned.1.call-start = ((), (), s32[]{:S(2)}) async-start(), calls=%async_computation.4 | async-start | bytes 4866048 | tf_op jit(solution)/shard_map/all_gather | solution.py:21
  8.7 360.0 %reduce-scatter.8.cloned.1.call-start = ((), (), s32[]{:S(2)}) async-start(), calls=%async_computation.5 | async-start | bytes 557056 | tf_op jit(solution)/shard_map/reduce_scatter | solution.py:81
  228.2 2.0 copy-start
  230.9 4.6 copy-start.1
  231.0 4.6 copy-start.5
  235.6 1.9 copy-start.7
  243.7 2.0 copy-start
  246.4 5.2 copy-start.1
  246.4 5.2 copy-start.5
  251.6 1.9 copy-start.7
  259.8 222.0 %reduce-scatter.10.cloned.1.call-start = ((), (), s32[]{:S(2)}) async-start(), calls=%async_computation.6 | async-start | bytes 1114112
  262.7 368.7 %reduce-scatter.12.cloned.1.call-start = ((), (), s32[]{:S(2)}) async-start(), calls=%async_computation.7 | async-start | bytes 1216512
  483.1 5.5 copy-start.10
  484.5 4.3 copy-start.8
  484.5 4.7 copy-start.3
  484.5 4.7 copy-start.6
  488.9 1.8 copy-start.4
Sparse Core Ops, SparseCore 0:
  10.2 71.3 all-gather.2
  83.7 72.3 all-gather.4
  259.9 108.7 reduce-scatter.7
  373.1 108.5 reduce-scatter.9
  484.7 146.6 reduce-scatter.11
where the time goes:
time: 733 us
  waiting for transfers between devices  356 us (49%)
  blocking collectives  296 us (40%)
  matrix products  41.3 us (6%)
  local copies, waits for them, and re-layouts  16.5 us (2%)
  between operations  14 us (2%)
  other arithmetic  8.75 us (1%)
    unnamed x7, waiting for transfers between devices  253 us
    reduce_scatter x1, waiting for transfers between devices, per_device(): lax.psum_scatter(key_terms.astype(jnp.bfloat16), 'seq', scatter_dimension...  102 us
    psum x1, blocking collectives, per_device(): weight_grad = lax.psum(row_share, 'seq').astype(jnp.float32)  93.3 us
    all_gather x1, blocking collectives, per_device(): lax.all_gather(values_local, 'seq', axis=0, tiled=True)  61 us
    all_gather x1, blocking collectives, per_device(): lax.all_gather(keys_local, 'seq', axis=0, tiled=True)  51.5 us
    all_gather x1, blocking collectives, per_device(): lax.all_gather(w_value, 'dp', axis=0, tiled=True)  50.2 us
    all_gather x1, blocking collectives, per_device(): lax.all_gather(w_key, 'dp', axis=0, tiled=True)  40.3 us
  transfers between devices with their start and end apart: 5, of which 3 were waited for; matrix products, arithmetic and copies ran while one was open for 3% of the time, Pallas kernels for 0%

commit v1 on v0

v1 whole, which is shorter than its diff:
```python
import functools
import jax
import jax.numpy as jnp
from jax import lax
from jax.experimental import pallas as pl
from jax.experimental.pallas import tpu as pltpu
from jax.sharding import PartitionSpec as P

MESH = pl.DeviceIdType.MESH
BF = jnp.bfloat16
F32 = jnp.float32
HEADS, HQ, DV = 8, 128, 192
COLS = 2944
SHARD = 48


def spot():
    dp, sq = lax.axis_index("dp"), lax.axis_index("seq")
    x, zl, c = lax.div(dp, 8), lax.div(lax.rem(dp, 8), 2), lax.rem(dp, 2)
    zh, y = lax.div(sq, 4), lax.rem(sq, 4)
    return x, y, zh * 4 + zl, c


def dev(dx=0, dy=0, dz=0, dc=0):
    x, y, z, c = spot()
    x, y = lax.rem(x + dx + 4, 4), lax.rem(y + dy + 4, 4)
    z, c = lax.rem(z + dz + 16, 16), lax.rem(c + dc, 2)
    return (x * 8 + lax.rem(z, 4) * 2 + c, lax.div(z, 4) * 4 + y)


AXES = {
    "x": ((1, 0, 0), (-1, 0, 0)),
    "y": ((0, 1, 0), (0, -1, 0)),
    "z": ((0, 0, 1), (0, 0, -1)),
    "w": ((0, 0, 4), (0, 0, -4)),
}


class Gather:
    def __init__(self, buf, row_of, rows, col, cols, halves, order, send, recv, base, twin=None):
        self.buf, self.row_of, self.rows, self.col, self.cols = buf, row_of, rows, col, cols
        self.halves, self.order, self.send, self.recv, self.base = halves, order, send, recv, base
        self.twin = twin

    def block(self, ka, kb, part=None):
        r0, nr, c0, nc = part if part else (0, self.rows, 0, self.cols)
        return self.buf.at[pl.ds(pl.multiple_of(self.row_of(ka, kb) + r0, 16), nr), pl.ds(self.col + c0, nc)]

    def copy(self, ka, kb, part, to, slot):
        ref = self.block(ka, kb, part)
        return pltpu.make_async_remote_copy(
            src_ref=ref, dst_ref=ref, send_sem=self.send, recv_sem=self.recv.at[self.base + slot],
            device_id=to, device_id_type=MESH)

    def put(self, ka, kb, part, axis, way, slot):
        if part is not None and (part[1] == 0 or part[3] == 0):
            return
        self.copy(ka, kb, part, dev(*AXES[self.order[axis]][way]), slot).start()

    def got(self, ka, kb, part, slot):
        if part is not None and (part[1] == 0 or part[3] == 0):
            return
        self.copy(ka, kb, part, dev(*AXES[self.order[0]][0]), slot).wait_recv()

    def share(self, ka, kb):
        if self.twin is None:
            return
        ref = self.block(ka, kb)
        pltpu.make_async_remote_copy(
            src_ref=ref, dst_ref=ref, send_sem=self.twin[0], recv_sem=self.twin[1],
            device_id=dev(0, 0, 0, 1), device_id_type=MESH).start()

    def first(self):
        self.put(0, 0, None, 0, 0, 0)
        self.put(0, 0, None, 0, 1, 1)
        self.second(0)
        self.share(0, 0)

    def second(self, k):
        self.put(k, 0, None, 1, 0, 4 + 4 * k)
        self.put(k, 0, None, 1, 1, 5 + 4 * k)

    def a_near(self, k, way):
        self.got(k, 0, None, 0 if k == 3 else 1)
        self.put(k, 0, self.halves[way], 0, way, 2 + way)
        self.second(k)
        self.share(k, 0)

    def a_far(self):
        self.got(2, 0, self.halves[0], 2)
        self.got(2, 0, self.halves[1], 3)
        self.second(2)
        self.share(2, 0)

    def b_near(self, k, kb, way):
        self.got(k, kb, None, 4 + 4 * k + (0 if kb == 3 else 1))
        self.put(k, kb, self.halves[way], 1, way, 6 + 4 * k + way)
        self.share(k, kb)

    def b_far(self, k):
        self.got(k, 2, self.halves[0], 6 + 4 * k)
        self.got(k, 2, self.halves[1], 7 + 4 * k)
        self.share(k, 2)

    def steps(self):
        near = lambda k: [lambda: self.b_near(k, 3, 0), lambda: self.b_near(k, 1, 1)]
        return ([self.first, lambda: self.a_near(3, 0), lambda: self.a_near(1, 1)] + near(0) + [self.a_far]
                + near(3) + near(1) + [lambda: self.b_far(0)] + near(2)
                + [lambda: self.b_far(3), lambda: self.b_far(1), lambda: self.b_far(2)])

    def settle(self):
        ref = self.buf.at[pl.ds(0, 16 * self.rows), pl.ds(self.col, self.cols)]
        pltpu.make_async_copy(ref, ref, self.twin[1]).wait()

    def drain(self):
        ref = self.buf.at[pl.ds(0, 15 * self.rows), pl.ds(self.col, self.cols)]
        pltpu.make_async_copy(ref, ref, self.send).wait()
        if self.twin is not None:
            ref = self.buf.at[pl.ds(0, 16 * self.rows), pl.ds(self.col, self.cols)]
            pltpu.make_async_copy(ref, ref, self.twin[0]).wait()


def col_halves(cols, rows, flip):
    lo = cols // 256 * 128
    if flip:
        lo = cols - lo
    return ((0, rows, 0, lo), (0, rows, lo, cols - lo))


PIECES = ((0, 128, "xz"), (128, 256, "zx"), (384, 384, "xz"), (768, 640, "zx"), (1408, 512, "xz"), (1920, 1024, "zx"))
PEERS = ((1, 0, 0), (-1, 0, 0), (2, 0, 0), (0, 1, 0), (0, -1, 0), (0, 2, 0), (0, 0, 1), (0, 0, -1), (0, 0, 2), (0, 0, -2),
         (0, 0, 4), (0, 0, -4), (0, 0, 8), (0, 0, 0, 1))


def nt(a, b):
    return lax.dot_general(a, b, (((1,), (1,)), ((), ())), preferred_element_type=F32)


def tn(a, b):
    return lax.dot_general(a, b, (((0,), (0,)), ((), ())), preferred_element_type=F32)


def gather_phase(act, gain, wq, wk, wv, wo, cot, wall, kv, normed, rs, q, g, sends, recvs, twins, ksend, krecv):
    barrier = pltpu.get_barrier_semaphore()
    for p in PEERS:
        pl.semaphore_signal(barrier, inc=1, device_id=dev(*p), device_id_type=MESH)
    x, y, z, c = spot()
    mine = pl.ds(pl.multiple_of(((x * 4 + lax.rem(z, 4)) * 2 + c) * SHARD, 16), SHARD)
    wall[mine, 0:128] = wk[...]
    wall[mine, 256:384] = jnp.zeros((SHARD, 128), BF)
    wall[mine, 128:320] = wv[...]
    wall[mine, 384:1408] = wq[...]
    wall[mine, 1408:2944] = wo[...]
    pl.semaphore_wait(barrier, len(PEERS))

    def row(order):
        def of(ka, kb):
            kx, kz = (ka, kb) if order == "xz" else (kb, ka)
            return ((lax.rem(x + kx, 4) * 4 + lax.rem(z + kz, 4)) * 2 + c) * SHARD
        return of

    parts = [Gather(wall, row(o), SHARD, c0, nc, col_halves(nc, SHARD, i % 2), o, sends.at[i], recvs, 20 * i,
                    (twins.at[0, i], twins.at[1, i])) for i, (c0, nc, o) in enumerate(PIECES)]

    def run(group):
        for line in zip(*[p.steps() for p in group]):
            for s in line:
                s()

    a = parts[0].steps(), parts[1].steps()
    for i in range(3):
        a[0][i](); a[1][i]()
    for p in parts[2:]:
        p.first()
    wide = act[...].astype(F32)
    r = lax.rsqrt(jnp.mean(wide * wide, axis=-1, keepdims=True) + 1e-6)
    rs[...] = r
    normed[...] = (wide * r * gain[...]).astype(BF)
    for i in range(3, len(a[0])):
        a[0][i](); a[1][i]()
    parts[0].settle(); parts[1].settle()
    both = jnp.dot(normed[...], wall[:, 0:320], preferred_element_type=F32).astype(BF)
    own = pl.ds(pl.multiple_of((lax.div(z, 4) * 4 + y) * 128, 128), 128)
    kv[own, 256:384] = jnp.zeros((128, 128), BF)
    kv[own, 0:320] = both

    def kv_row(ka, kb):
        return (lax.rem(lax.div(z, 4) + ka, 4) * 4 + lax.rem(y + kb, 4)) * 128

    kvg = Gather(kv, kv_row, 128, 0, 384, ((0, 64, 0, 384), (64, 64, 0, 384)), "wy", ksend, krecv, 0)
    ks = kvg.steps()
    bulk = [p.steps()[1:] for p in parts[2:]]
    ks[0]()
    for i in range(len(bulk[0])):
        for b in bulk:
            b[i]()
        ks[i + 1]()
    parts[2].settle(); parts[3].settle()
    qs = (jnp.dot(normed[...], wall[:, 384:1408], preferred_element_type=F32) * HQ ** -0.5).astype(BF)
    for h in range(HEADS):
        q[pl.ds(h * 128, 128), :] = qs[:, h * HQ:(h + 1) * HQ]
    parts[4].settle(); parts[5].settle()
    for h in range(HEADS):
        g[pl.ds(h * 128, 128), :] = nt(cot[...], wall[pl.ds(h * DV, DV), 1408:2944]).astype(BF)
    for p in parts:
        p.drain()
    kvg.drain()


def softmax_phase(q, g, kv, e, vt, gt, att, inv, centre):
    vt[...] = kv[:, 128:320].T
    gt[...] = g[...].T
    wide = 512

    @pl.loop(0, 1024 // wide)
    def _(i):
        at = pl.ds(pl.multiple_of(i * wide, wide), wide)
        s = nt(kv[:, 0:128], q[at, :])
        p = jnp.exp(s - jnp.max(s, axis=0, keepdims=True))
        r = 1.0 / jnp.sum(p, axis=0, keepdims=True)
        pb = p.astype(BF)
        e[:, at] = pb
        a = jnp.dot(vt[...], pb, preferred_element_type=F32) * r
        att[:, at] = a.astype(BF)
        inv[:, at] = r
        centre[:, at] = jnp.sum(a * gt[:, at].astype(F32), axis=0, keepdims=True)


def grads_of(rows, q, g, kv, e, inv, centre, part, dqt, start):
    dp = nt(kv[rows, 128:320], g[...])
    p = e[rows, :].astype(F32) * inv[...]
    part[rows, 128:320] = jnp.dot(p.astype(BF), g[...], preferred_element_type=F32).astype(BF)
    ds = (p * (dp - centre[...])).astype(BF)
    part[rows, 0:128] = jnp.dot(ds, q[...], preferred_element_type=F32).astype(BF)
    term = tn(kv[rows, 0:128], ds)
    if start:
        dqt[...] = term
    else:
        dqt[...] += term


def body(act, gain, wq, wk, wv, wo, cot, out, ingrad, wgrad,
         wall, kv, normed, rs, q, g, e, vt, gt, att, inv, centre, part, dqt, rows_of, ng,
         ybuf, zsend, zbuf, wg, cbuf, xs, xbuf, ys, ybuf2, zs, zbuf2, hs, hbuf, last,
         sends, recvs, twins, ksend, krecv, ysem, zsem, wsem):
    part[:, 256:384] = jnp.zeros((2048, 128), BF)
    gather_phase(act, gain, wq, wk, wv, wo, cot, wall, kv, normed, rs, q, g, sends, recvs, twins, ksend, krecv)
    softmax_phase(q, g, kv, e, vt, gt, att, inv, centre)
    x, y, z, c = spot()
    zh, zl = lax.div(z, 4), lax.rem(z, 4)
    wide = lambda ref: ref.astype(F32)

    def send(src, dst, sems, to):
        cp = pltpu.make_async_remote_copy(src_ref=src, dst_ref=dst, send_sem=sems.at[0], recv_sem=sems.at[1],
                                          device_id=to, device_id_type=MESH)
        cp.start()
        return cp

    def group(k):
        return lax.rem(zh + k, 4) * 512

    def block(k, dy):
        return pl.ds(pl.multiple_of(group(k) + lax.rem(y + dy, 4) * 128, 128), 128)

    yc, zc = {}, {}

    def out_y(k):
        yc[k] = [send(part.at[block(k, dy)], ybuf.at[k, dy - 1], ysem.at[k, dy - 1], dev(0, dy)) for dy in (1, 3, 2)]

    def out_z(k):
        for cp in yc[k]:
            cp.wait()
        zsend[k] = (wide(part[block(k, 0), :]) + wide(ybuf[k, 0]) + wide(ybuf[k, 1]) + wide(ybuf[k, 2])).astype(BF)
        if k:
            zc[k] = send(zsend.at[k], zbuf.at[k - 1], zsem.at[k - 1], dev(0, 0, 4 * k))

    previous = None
    for k in (2, 1, 3, 0):
        grads_of(pl.ds(pl.multiple_of(group(k), 512), 512), q, g, kv, e, inv, centre, part, dqt, k == 2)
        out_y(k)
        if previous is not None:
            out_z(previous)
        previous = k
    for h in range(HEADS):
        rows_of[:, h * HQ:(h + 1) * HQ] = (dqt[:, h * 128:(h + 1) * 128].T * HQ ** -0.5).astype(BF)
    ng[...] = nt(rows_of[:, 0:1024], wall[:, 384:1408])
    out_z(0)
    for k in (1, 2, 3):
        zc[k].wait()
    kvg = (wide(zsend[0]) + wide(zbuf[0]) + wide(zbuf[1]) + wide(zbuf[2])).astype(BF)

    wg[...] = tn(normed[...], kvg).astype(BF).reshape(4, 4, 2, SHARD, 384)
    cp = send(wg.at[:, :, 1 - c], cbuf, wsem.at[0], dev(0, 0, 0, 1))
    scaled = (ng[...] + nt(kvg[:, 0:320], wall[:, 0:320])) * gain[...]
    cp.wait()
    xs[...] = (wide(wg[:, :, c]) + wide(cbuf[...])).astype(BF)
    cps = [send(xs.at[lax.rem(x + d, 4)], xbuf.at[d - 1], wsem.at[d], dev(d)) for d in (1, 3, 2)]
    a, r = wide(act[...]), rs[...]
    inner = jnp.mean(scaled * a, axis=-1, keepdims=True)
    ingrad[...] = (wide(cot[...]) + r * (scaled - a * r * r * inner)).astype(BF)
    for h in range(0, HEADS, 2):
        pair = att[:, h * 128:(h + 2) * 128].T
        rows_of[:, h * DV:(h + 2) * DV] = jnp.concatenate([pair[:128], pair[128:]], axis=1)
    for cp in cps:
        cp.wait()
    ys[...] = (wide(xs[x]) + wide(xbuf[0]) + wide(xbuf[1]) + wide(xbuf[2])).astype(BF)
    cps = [send(ys.at[lax.rem(y + d, 4)], ybuf2.at[d - 1], wsem.at[3 + d], dev(0, d)) for d in (1, 3, 2)]
    half = 768
    out[:, 0:half] = (wide(act[:, 0:half]) + jnp.dot(rows_of[...], wall[:, 1408:1408 + half], preferred_element_type=F32)).astype(BF)
    for cp in cps:
        cp.wait()
    zs[...] = (wide(ys[y]) + wide(ybuf2[0]) + wide(ybuf2[1]) + wide(ybuf2[2])).astype(BF)
    turn = lax.rem(y - zl + 4, 4)
    for t in (1, 2, 3):
        @pl.when(turn == t)
        def _():
            send(zs, zbuf2.at[t - 1], wsem.at[6 + t], dev(0, 0, t if t < 3 else -1)).wait_send()
    out[:, half:] = (wide(act[:, half:]) + jnp.dot(rows_of[...], wall[:, 1408 + half:], preferred_element_type=F32)).astype(BF)

    @pl.when(turn == 0)
    def _():
        for t in (1, 2, 3):
            pltpu.make_async_copy(zs, zbuf2.at[t - 1], wsem.at[6 + t, 1]).wait()
        hs[...] = (wide(zs[...]) + wide(zbuf2[0]) + wide(zbuf2[1]) + wide(zbuf2[2])).astype(BF)
        for cp in [send(hs, hbuf.at[k - 1], wsem.at[9 + k], dev(0, 0, 4 * k)) for k in (2, 1, 3)]:
            cp.wait()
        last[...] = (wide(hs[...]) + wide(hbuf[0]) + wide(hbuf[1]) + wide(hbuf[2])).astype(BF)
        for cp in [send(last, last, wsem.at[12 + d], dev(0, d)) for d in (1, 3, 2)]:
            cp.wait_send()

    for d in (1, 2, 3):
        @pl.when(lax.rem(zl + d, 4) == y)
        def _():
            pltpu.make_async_copy(last, last, wsem.at[12 + d, 1]).wait()
    wgrad[...] = wide(last[:, 0:320])


def per_device(act, gain, wq, wk, wv, wo, cot):
    vm = pl.BlockSpec(memory_space=pltpu.VMEM)
    V, DMA = pltpu.VMEM, pltpu.SemaphoreType.DMA
    scratch = [
        V((1536, COLS), BF), V((2048, 384), BF), V((128, 1536), BF), V((128, 1), F32), V((1024, 128), BF), V((1024, 192), BF),
        V((2048, 1024), BF), V((192, 2048), BF), V((192, 1024), BF), V((192, 1024), BF), V((1, 1024), F32), V((1, 1024), F32),
        V((2048, 384), BF), V((128, 1024), F32), V((128, 1536), BF), V((128, 1536), F32),
        V((4, 3, 128, 384), BF), V((4, 128, 384), BF), V((3, 128, 384), BF), V((4, 4, 2, SHARD, 384), BF),
        V((4, 4, SHARD, 384), BF), V((4, 4, SHARD, 384), BF), V((3, 4, SHARD, 384), BF), V((4, SHARD, 384), BF),
        V((3, SHARD, 384), BF), V((SHARD, 384), BF), V((3, SHARD, 384), BF), V((SHARD, 384), BF), V((3, SHARD, 384), BF),
        V((SHARD, 384), BF),
        DMA((6,)), DMA((120,)), DMA((2, 6)), DMA, DMA((20,)), DMA((4, 3, 2)), DMA((3, 2)), DMA((16, 2)),
    ]
    o, i, w = pl.pallas_call(
        body,
        out_shape=(jax.ShapeDtypeStruct((128, 1536), BF), jax.ShapeDtypeStruct((128, 1536), BF),
                   jax.ShapeDtypeStruct((SHARD, 320), F32)),
        in_specs=[vm] * 7, out_specs=(vm,) * 3, scratch_shapes=scratch,
        compiler_params=pltpu.CompilerParams(collective_id=0, has_side_effects=True, vmem_limit_bytes=58 * 2**20),
        name="layer",
    )(act[0], gain.reshape(1, -1), wq, wk, wv, wo, cot[0])
    return o[None], i[None], w


def solution(mesh):
    rows = P("dp", "seq", None)
    split = P("dp", None)
    return jax.shard_map(per_device, mesh=mesh, in_specs=(rows, P(), split, split, split, split, rows),
                         out_specs=(rows, rows, split), check_vma=False)
```

time: 733 us -> 142 us (0.19)
  waiting for transfers between devices: 356 us -> 0 us
  blocking collectives: 296 us -> 0 us
  Pallas kernels: 0 us -> 136 us
  matrix products: 41.3 us -> 0 us
  between operations: 14 us -> 0.65 us
  local copies, waits for them, and re-layouts: 16.5 us -> 4.68 us
  other arithmetic: 8.75 us -> 0 us
    unnamed x7 -> x0, waiting for transfers between devices: 253 us -> none
    all_gather x4 -> x0, blocking collectives: 203 us -> none  [the longest x1 61 us: per_device(): lax.all_gather(values_local, 'seq', axis=0, tiled=True)]
    pallas_call x0 -> x1, Pallas kernels: none -> 136 us  [per_device(): pl.pallas_call(body, out_shape=(jax.ShapeDtypeStruct((128, 1536), BF), ja...]
    reduce_scatter x1 -> x0, waiting for transfers between devices: 102 us -> none  [per_device(): lax.psum_scatter(key_terms.astype(jnp.bfloat16), 'seq', scatter_dimension...]
    psum x1 -> x0, blocking collectives: 93.3 us -> none  [per_device(): weight_grad = lax.psum(row_share, 'seq').astype(jnp.float32)]
    dot_general x22 -> x0, matrix products: 41.3 us -> none  [the longest x2 9.73 us: block_pass(): jnp.dot(probs_b.T, grad_block, preferred_element_type=jnp.float32)]
  transfers between devices with their start and end apart: 5 -> 0, of which waited for: 3 -> 0; matrix products, arithmetic and copies ran while one was open for 3% -> 0% of each run, Pallas kernels for 0% -> 0%
where the time goes in v1:
time: 142 us
  Pallas kernels  136 us (96%)
  local copies, waits for them, and re-layouts  4.68 us (3%)
    pallas_call x1, Pallas kernels, per_device(): pl.pallas_call(body, out_shape=(jax.ShapeDtypeStruct((128, 1536), BF), ja...  136 us
    unnamed x7, local copies, waits for them, and re-layouts  3.38 us

profile of v1, /device:TPU:16, one launch (start us, length us, event | category | flops | bytes accessed | tf_op | source)
XLA Modules:
  0.0 141.6 jit_solution(16976120907871604597)
XLA Ops:
  0.6 1.3 reshape.9.gain
  1.9 136.3 %layer.1 = (bf16[128,1536]{1,0:T(8,128)(2,1)}, bf16[128,1536]{1,0:T(8,128)(2,1)}, f32[48,320]{1,0:T(8,128)}) custom-call(bf16[128,1536]{1,0:T(8,128)(2,1)} %bitcast.4, f32[1,1536]{1,0:T(1,128)} %reshape.9.gain, bf16[48,1024]{1,0:T(8,128)(2,1)} %wq.1, bf16[48,128]{1,0:T(8,128)(2,1)} %wk.1, bf16[48,192]{1,0:T(8,128)(2,1)} %wv.1, bf16[48,1536]{1,0:T(8,128)(2,1)} %wo.1, ...), custom_call_target="tpu_custom_call" | custom-call | tf_op jit(solution)/shard_map/layer/pallas_call | solution.py:351
  138.2 0.0 copy-start
  138.2 1.8 %copy.13 = bf16[1,128,1536]{2,1,0:T(8,128)(2,1)} copy(bf16[1,128,1536]{2,1,0:T(8,128)(2,1)} %bitcast.7) | data formatting | bytes 786432
  140.0 0.0 copy-done
  140.1 0.0 copy-start.1
  140.1 0.7 copy.14
  140.8 0.2 copy-done.1
  141.0 0.6 copy.15
Async XLA Ops:
  138.2 1.8 %copy-start = (bf16[128,1536]{1,0:T(8,128)(2,1)S(1)}, bf16[128,1536]{1,0:T(8,128)(2,1)}, u32[]{:S(2)}) copy-start(bf16[128,1536]{1,0:T(8,128)(2,1)} %get-tuple-element.7) | copy-start | bytes 1179652
  140.1 0.9 copy-start.1

commit v2 on v1

v2 whole, which is shorter than its diff:
```python
import functools
import jax
import jax.numpy as jnp
from jax import lax
from jax.experimental import pallas as pl
from jax.experimental.pallas import tpu as pltpu
from jax.sharding import PartitionSpec as P

MESH = pl.DeviceIdType.MESH
BF = jnp.bfloat16
F32 = jnp.float32
HEADS, HQ, DV = 8, 128, 192
COLS = 2944
SHARD = 48


def spot():
    dp, sq = lax.axis_index("dp"), lax.axis_index("seq")
    x, zl, c = lax.div(dp, 8), lax.div(lax.rem(dp, 8), 2), lax.rem(dp, 2)
    zh, y = lax.div(sq, 4), lax.rem(sq, 4)
    return x, y, zh * 4 + zl, c


def dev(dx=0, dy=0, dz=0, dc=0):
    x, y, z, c = spot()
    x, y = lax.rem(x + dx + 4, 4), lax.rem(y + dy + 4, 4)
    z, c = lax.rem(z + dz + 16, 16), lax.rem(c + dc, 2)
    return (x * 8 + lax.rem(z, 4) * 2 + c, lax.div(z, 4) * 4 + y)


AXES = {
    "x": ((1, 0, 0), (-1, 0, 0)),
    "y": ((0, 1, 0), (0, -1, 0)),
    "z": ((0, 0, 1), (0, 0, -1)),
}


class Gather:
    def __init__(self, buf, row_of, rows, col, cols, halves, order, send, recv, base, twin=None, direct=False):
        self.buf, self.row_of, self.rows, self.col, self.cols = buf, row_of, rows, col, cols
        self.halves, self.order, self.send, self.recv, self.base = halves, order, send, recv, base
        self.twin, self.direct = twin, direct

    def block(self, ka, kb, part=None):
        r0, nr, c0, nc = part if part else (0, self.rows, 0, self.cols)
        return self.buf.at[pl.ds(pl.multiple_of(self.row_of(ka, kb) + r0, 16), nr), pl.ds(self.col + c0, nc)]

    def copy(self, ka, kb, part, to, slot):
        ref = self.block(ka, kb, part)
        return pltpu.make_async_remote_copy(
            src_ref=ref, dst_ref=ref, send_sem=self.send, recv_sem=self.recv.at[self.base + slot],
            device_id=to, device_id_type=MESH)

    def put(self, ka, kb, part, axis, way, slot):
        if part is not None and (part[1] == 0 or part[3] == 0):
            return
        self.copy(ka, kb, part, dev(*AXES[self.order[axis]][way]), slot).start()

    def far(self, k, axis, slot):
        if self.direct:
            self.copy(k, 0, None, dev(*[2 * d for d in AXES[self.order[axis]][0]]), slot).start()

    def got(self, ka, kb, part, slot):
        if part is not None and (part[1] == 0 or part[3] == 0):
            return
        self.copy(ka, kb, part, dev(*AXES[self.order[0]][0]), slot).wait_recv()

    def share(self, ka, kb):
        if self.twin is None:
            return
        ref = self.block(ka, kb)
        pltpu.make_async_remote_copy(
            src_ref=ref, dst_ref=ref, send_sem=self.twin[0], recv_sem=self.twin[1],
            device_id=dev(0, 0, 0, 1), device_id_type=MESH).start()

    def first(self):
        self.put(0, 0, None, 0, 0, 0)
        self.put(0, 0, None, 0, 1, 1)
        self.far(0, 0, 2)
        self.second(0)
        self.share(0, 0)

    def second(self, k):
        self.put(k, 0, None, 1, 0, 4 + 4 * k)
        self.put(k, 0, None, 1, 1, 5 + 4 * k)
        self.far(k, 1, 6 + 4 * k)

    def a_near(self, k, way):
        self.got(k, 0, None, 0 if k == 3 else 1)
        if not self.direct:
            self.put(k, 0, self.halves[way], 0, way, 2 + way)
        self.second(k)
        self.share(k, 0)

    def a_far(self):
        if self.direct:
            self.got(2, 0, None, 2)
        else:
            self.got(2, 0, self.halves[0], 2)
            self.got(2, 0, self.halves[1], 3)
        self.second(2)
        self.share(2, 0)

    def b_near(self, k, kb, way):
        self.got(k, kb, None, 4 + 4 * k + (0 if kb == 3 else 1))
        if not self.direct:
            self.put(k, kb, self.halves[way], 1, way, 6 + 4 * k + way)
        self.share(k, kb)

    def b_far(self, k):
        if self.direct:
            self.got(k, 2, None, 6 + 4 * k)
        else:
            self.got(k, 2, self.halves[0], 6 + 4 * k)
            self.got(k, 2, self.halves[1], 7 + 4 * k)
        self.share(k, 2)

    def steps(self):
        near = lambda k: [lambda: self.b_near(k, 3, 0), lambda: self.b_near(k, 1, 1)]
        return ([self.first, lambda: self.a_near(3, 0), lambda: self.a_near(1, 1)] + near(0) + [self.a_far]
                + near(3) + near(1) + [lambda: self.b_far(0)] + near(2)
                + [lambda: self.b_far(3), lambda: self.b_far(1), lambda: self.b_far(2)])

    def settle(self):
        ref = self.buf.at[pl.ds(0, 16 * self.rows), pl.ds(self.col, self.cols)]
        pltpu.make_async_copy(ref, ref, self.twin[1]).wait()

    def drain(self):
        ref = self.buf.at[pl.ds(0, 15 * self.rows), pl.ds(self.col, self.cols)]
        pltpu.make_async_copy(ref, ref, self.send).wait()
        if self.twin is not None:
            ref = self.buf.at[pl.ds(0, 16 * self.rows), pl.ds(self.col, self.cols)]
            pltpu.make_async_copy(ref, ref, self.twin[0]).wait()


def col_halves(cols, rows, flip):
    lo = cols // 256 * 128
    if flip:
        lo = cols - lo
    return ((0, rows, 0, lo), (0, rows, lo, cols - lo))


PIECES = ((0, 128, "xz"), (128, 256, "zx"), (384, 384, "xz"), (768, 640, "zx"), (1408, 512, "xz"), (1920, 1024, "zx"))
PLANE = [(dx, 0, dz) for dx in (0, 1, -1, 2) for dz in (0, 1, -1, 2)][1:]
PEERS = [(2, 0, -2), (1, 0, -2), (-1, 0, -2), (0, 0, -2)] + PLANE + [
    (0, 1, 0), (0, -1, 0), (0, 2, 0), (0, 0, 4), (0, 0, -4), (0, 0, 8), (0, 0, 0, 1)]


def nt(a, b):
    return lax.dot_general(a, b, (((1,), (1,)), ((), ())), preferred_element_type=F32)


def tn(a, b):
    return lax.dot_general(a, b, (((0,), (0,)), ((), ())), preferred_element_type=F32)


def hello():
    barrier = pltpu.get_barrier_semaphore()
    for p in PEERS:
        pl.semaphore_signal(barrier, inc=1, device_id=dev(*p), device_id_type=MESH)
    return barrier


def remote(src, dst, send, recv, to):
    return pltpu.make_async_remote_copy(src_ref=src, dst_ref=dst, send_sem=send, recv_sem=recv, device_id=to,
                                        device_id_type=MESH)


def pack(v):
    return jnp.concatenate([v[..., :64, :], v[..., 64:, :]], axis=-1)


def unpack(w):
    return jnp.concatenate([w[..., :64], w[..., 64:]], axis=-2)


class Window:
    def __init__(self, buf, sends, recvs):
        self.buf, self.sends, self.recvs = buf, sends, recvs

    def at(self, kz, half=None):
        x, y, z, c = spot()
        b = self.buf.at[lax.rem(lax.div(z, 4) + kz, 4) * 4 + y]
        return b if half is None else b.at[pl.ds(160 * half, 160)]

    def hop(self, kz, half, up, slot):
        ref = self.at(kz, half)
        return remote(ref, ref, self.sends.at[slot], self.recvs.at[slot], dev(0, 0, 4 if up else -4))

    def across(self, kz, half, dy):
        ref, slot = self.at(kz, half), 6 + (kz * 2 + half) * 3 + dy - 1
        return remote(ref, ref, self.sends.at[slot], self.recvs.at[slot], dev(0, dy))

    def row(self, kz, half):
        for dy in (1, 3, 2):
            self.across(kz, half, dy).start()

    def got(self, kz, half, slot):
        self.hop(kz, half, True, slot).wait_recv()

    def steps(self):
        def s0():
            self.hop(0, 0, True, 0).start()
            self.hop(0, 1, False, 1).start()
            self.hop(0, 1, True, 2).start()
            self.hop(0, 0, False, 3).start()
            self.row(0, 0)
            self.row(0, 1)

        def s1():
            self.got(3, 0, 0)
            self.hop(3, 0, True, 4).start()
            self.row(3, 0)

        def s2():
            self.got(1, 1, 1)
            self.hop(1, 1, False, 5).start()
            self.row(1, 1)

        def s3():
            self.got(3, 1, 2)
            self.row(3, 1)

        def s4():
            self.got(1, 0, 3)
            self.row(1, 0)

        def s5():
            self.got(2, 0, 4)
            self.row(2, 0)
            self.got(2, 1, 5)
            self.row(2, 1)

        def s6():
            for kz, half in ((0, 0), (0, 1), (3, 0), (1, 1), (3, 1), (1, 0), (2, 0), (2, 1)):
                for dy in (1, 3, 2):
                    self.across(kz, half, dy).wait_recv()

        return [s0, s1, s2, s3, s4, s5, s6]

    def drain(self):
        for slot in range(30):
            ref = self.at(0, 0)
            remote(ref, ref, self.sends.at[slot], self.recvs.at[slot], dev(0, 1)).wait_send()


def gather_phase(act, gain, wq, wk, wv, wo, cot, wall, kvp, normed, rs, q, sends, recvs, twins, ksend, krecv):
    barrier = hello()
    x, y, z, c = spot()
    mine = pl.ds(pl.multiple_of(((x * 4 + lax.rem(z, 4)) * 2 + c) * SHARD, 16), SHARD)
    wall[mine, 0:128] = wk[...]
    wall[mine, 256:384] = jnp.zeros((SHARD, 128), BF)
    wall[mine, 128:320] = wv[...]
    wall[mine, 384:1408] = wq[...]
    wall[mine, 1408:2944] = wo[...]
    wide = act[...].astype(F32)
    r = lax.rsqrt(jnp.mean(wide * wide, axis=-1, keepdims=True) + 1e-6)
    rs[...] = r
    normed[...] = (wide * r * gain[...][None, :]).astype(BF)
    pl.semaphore_wait(barrier, len(PEERS))

    def row(order):
        def of(ka, kb):
            kx, kz = (ka, kb) if order == "xz" else (kb, ka)
            return ((lax.rem(x + kx, 4) * 4 + lax.rem(z + kz, 4)) * 2 + c) * SHARD
        return of

    parts = [Gather(wall, row(o), SHARD, c0, nc, col_halves(nc, SHARD, i % 2), o, sends.at[i], recvs, 20 * i,
                    (twins.at[0, i], twins.at[1, i]), i < 2) for i, (c0, nc, o) in enumerate(PIECES)]
    kvs = [p.steps() for p in parts[:2]]
    bulk = [p.steps() for p in parts[2:]]

    def do(group, i):
        for steps in group:
            steps[i]()

    do(kvs, 0)
    for i in (1, 2, 5):
        do(kvs, i)
    do(bulk, 0)
    for i in (3, 4, 6, 7, 8, 9, 10, 11, 12, 13, 14, 15):
        do(kvs, i)
    parts[0].settle(); parts[1].settle()
    both = jnp.dot(normed[...], wall[:, 0:320], preferred_element_type=F32).astype(BF)
    own = lax.div(z, 4) * 4 + y
    kvp[own, 0:128, :] = both[:, 0:128]
    kvp[own, 128:256, :] = both[:, 128:256]
    kvp[own, 256:320, :] = pack(both[:, 256:320])
    win = Window(kvp, ksend, krecv)
    ks = win.steps()
    ks[0]()
    do(bulk, 1); do(bulk, 2); do(bulk, 3); do(bulk, 4); do(bulk, 5)
    ks[1](); ks[2]()
    do(bulk, 6); do(bulk, 7)
    ks[3](); ks[4]()
    do(bulk, 8); do(bulk, 9); do(bulk, 10)
    ks[5]()
    do(bulk, 11); do(bulk, 12); do(bulk, 13); do(bulk, 14); do(bulk, 15)
    parts[2].settle(); parts[3].settle()
    qs = (jnp.dot(normed[...], wall[:, 384:1408], preferred_element_type=F32) * HQ ** -0.5).astype(BF)
    for h in range(HEADS):
        q[pl.ds(h * 128, 128), :] = qs[:, h * HQ:(h + 1) * HQ]
    ks[6]()

    def finish():
        parts[4].settle(); parts[5].settle()
        for p in parts:
            p.drain()
        win.drain()
    return finish


def keys_of(kvp, first, n):
    return kvp[pl.ds(first, n), 0:128, :].reshape(n * 128, 128)


def softmax_phase(q, kvp, v, e, vt, att, inv):
    v[:, 0:128] = kvp[:, 128:256, :].reshape(2048, 128)
    v[:, 128:192] = unpack(kvp[:, 256:320, :]).reshape(2048, 64)
    vt[...] = v[...].T
    wide = 512

    @pl.loop(0, 1024 // wide)
    def _(i):
        at = pl.ds(pl.multiple_of(i * wide, wide), wide)
        s = nt(keys_of(kvp, 0, 16), q[at, :])
        p = jnp.exp(s - jnp.max(s, axis=0, keepdims=True))
        r = 1.0 / jnp.sum(p, axis=0, keepdims=True)
        pb = p.astype(BF)
        e[:, at] = pb
        att[:, at] = jnp.dot(vt[...], pb, preferred_element_type=F32) * r
        inv[:, at] = r


def value_terms(first, g, e, inv, part):
    rows = pl.ds(pl.multiple_of(first * 128, 512), 512)
    p = (e[rows, :].astype(F32) * inv[...]).astype(BF)
    dv = jnp.dot(p, g[...], preferred_element_type=F32).astype(BF).reshape(4, 128, 192)
    part[pl.ds(first, 4), 0:128, :] = dv[:, :, 0:128]
    part[pl.ds(first, 4), 128:192, :] = pack(dv[:, :, 128:192])


def key_terms(first, q, g, kvp, v, e, inv, centre, part, dqt, start):
    rows = pl.ds(pl.multiple_of(first * 128, 512), 512)
    dp = nt(v[rows, :], g[...])
    ds = (e[rows, :].astype(F32) * inv[...] * (dp - centre[...])).astype(BF)
    part[pl.ds(first, 4)] = jnp.dot(ds, q[...], preferred_element_type=F32).astype(BF).reshape(4, 128, 128)
    term = tn(keys_of(kvp, first, 4), ds)
    if start:
        dqt[...] = term
    else:
        dqt[...] += term


def post(src, dst, sems, to):
    cp = remote(src, dst, sems.at[0], sems.at[1], to)
    cp.start()
    return cp


class Total:
    def __init__(self, part, ybuf, zs, mid, fbuf, zbuf, wg, cbuf, xs, xbuf, ps, pbuf, hs, hbuf, sems):
        self.part, self.ybuf, self.zs, self.mid, self.fbuf, self.zbuf = part, ybuf, zs, mid, fbuf, zbuf
        self.wg, self.cbuf, self.xs, self.xbuf, self.ps, self.pbuf = wg, cbuf, xs, xbuf, ps, pbuf
        self.hs, self.hbuf, self.sems = hs, hbuf, sems
        self.rows = part.shape[1]
        self.x, self.y, self.z, self.c = spot()
        self.zh, self.zl = lax.div(self.z, 4), lax.rem(self.z, 4)
        self.yc, self.zc = {}, []

    def group(self, k):
        return lax.rem(self.zh + k, 4) * 4

    def y_out(self, k):
        self.yc[k] = [post(self.part.at[self.group(k) + lax.rem(self.y + dy, 4)], self.ybuf.at[k, dy - 1],
                           self.sems.at[k * 3 + dy - 1], dev(0, dy)) for dy in (1, 3, 2)]

    def y_in(self, k):
        for cp in self.yc[k]:
            cp.wait()
        f = lambda t: t.astype(F32)
        self.zs[k] = (f(self.part[self.group(k) + self.y]) + f(self.ybuf[k, 0]) + f(self.ybuf[k, 1]) + f(self.ybuf[k, 2])).astype(BF)
        half = self.rows // 2
        low, high = pl.ds(0, half), pl.ds(half, half)
        if k == 2:
            self.fc = [post(self.zs.at[2, low], self.fbuf.at[0], self.sems.at[12], dev(0, 0, 4)),
                       post(self.zs.at[2, high], self.fbuf.at[1], self.sems.at[13], dev(0, 0, -4))]
        if k == 1:
            self.zc.append(post(self.zs.at[1, high], self.zbuf.at[0, high], self.sems.at[14], dev(0, 0, 4)))
        if k == 3:
            self.zc.append(post(self.zs.at[3, low], self.zbuf.at[1, low], self.sems.at[15], dev(0, 0, -4)))

    def z_mid(self, way):
        half = self.rows // 2
        rows = pl.ds(half * way, half)
        self.fc[way].wait()
        self.mid[way] = (self.zs[3 if way else 1, rows].astype(F32) + self.fbuf[way].astype(F32)).astype(BF)
        self.zc.append(post(self.mid.at[way], self.zbuf.at[way, rows], self.sems.at[16 + way], dev(0, 0, -4 if way else 4)))

    def z_in(self):
        for cp in self.zc:
            cp.wait()
        return (self.zs[0].astype(F32) + self.zbuf[0].astype(F32) + self.zbuf[1].astype(F32)).astype(BF)

    def t0(self, normed, grad):
        self.wg[...] = tn(normed[...], grad).astype(BF).reshape(self.wg.shape)
        self.cps = [post(self.wg.at[:, :, 1 - self.c], self.cbuf, self.sems.at[18], dev(0, 0, 0, 1))]

    def wait(self):
        for cp in self.cps:
            cp.wait()

    def t1(self):
        self.wait()
        self.xs[...] = (self.wg[:, :, self.c].astype(F32) + self.cbuf[...].astype(F32)).astype(BF)
        self.cps = [post(self.xs.at[lax.rem(self.x + dx + 4, 4), lax.rem(self.zl + dz + 4, 4)], self.xbuf.at[i],
                         self.sems.at[19 + i], dev(dx, 0, dz)) for i, (dx, _, dz) in enumerate(PLANE)]

    def t2(self):
        self.wait()
        total = self.xs[self.x, self.zl].astype(F32)
        for i in range(15):
            total += self.xbuf[i].astype(F32)
        self.ps[...] = total.astype(BF)
        self.cps = [post(self.ps, self.pbuf.at[k - 1], self.sems.at[33 + k], dev(0, 0, 4 * k)) for k in (2, 1, 3)]

    def t3(self):
        self.wait()
        self.hs[...] = in_order(self.ps, self.pbuf, self.zh).astype(BF)
        self.cps = [post(self.hs, self.hbuf.at[d - 1], self.sems.at[36 + d], dev(0, d)) for d in (1, 3, 2)]

    def t4(self):
        self.wait()
        return in_order(self.hs, self.hbuf, self.y)


def in_order(mine, others, place):
    total = None
    for i in range(4):
        d = lax.rem(place - i + 4, 4)
        term = mine[...].astype(F32)
        for j in (1, 2, 3):
            term = jnp.where(d == j, others[j - 1].astype(F32), term)
        total = term if total is None else total + term
    return total


def body(act, gain, wq, wk, wv, wo, cot, out, ingrad, wgrad,
         wall, kvp, normed, rs, q, g, v, e, vt, att, inv, centre, dqt, rows_of, ng,
         sends, recvs, twins, ksend, krecv, *slabs):
    finish = gather_phase(act, gain, wq, wk, wv, wo, cot, wall, kvp, normed, rs, q, sends, recvs, twins, ksend, krecv)
    softmax_phase(q, kvp, v, e, vt, att, inv)
    finish()
    for h in range(HEADS):
        g[pl.ds(h * 128, 128), :] = nt(cot[...], wall[pl.ds(h * DV, DV), 1408:2944]).astype(BF)
    half = len(slabs) // 2
    K, V = Total(*slabs[:half]), Total(*slabs[half:])

    for k in (2, 1, 3, 0):
        value_terms(V.group(k), g, e, inv, V.part)
        V.y_out(k)
    centre[...] = jnp.sum(att[...] * g[...].astype(F32).T, axis=0, keepdims=True)
    for k in (2, 1, 3, 0):
        key_terms(K.group(k), q, g, kvp, v, e, inv, centre, K.part, dqt, k == 2)
        K.y_out(k)
        if k != 0:
            V.y_in(k)
    for h in range(HEADS):
        rows_of[:, h * HQ:(h + 1) * HQ] = (dqt[:, h * 128:(h + 1) * 128].T * HQ ** -0.5).astype(BF)
    ng[...] = nt(rows_of[:, 0:1024], wall[:, 384:1408])
    V.z_mid(0)
    V.z_mid(1)
    V.y_in(0)
    K.y_in(2)
    K.y_in(1)
    K.y_in(3)
    vsum = V.z_in()
    vgrad = jnp.concatenate([vsum[0:128], unpack(vsum[128:192])], axis=1)
    V.t0(normed, jnp.concatenate([vgrad, jnp.zeros((128, 64), BF)], axis=1))
    K.z_mid(0)
    K.z_mid(1)
    V.t1()
    K.y_in(0)
    kgrad = K.z_in()
    K.t0(normed, kgrad)
    scaled = (ng[...] + nt(jnp.concatenate([kgrad, vgrad], axis=1), wall[:, 0:320])) * gain[...][None, :]
    K.t1()
    a, r = act[...].astype(F32), rs[...]
    inner = jnp.mean(scaled * a, axis=-1, keepdims=True)
    ingrad[...] = (cot[...].astype(F32) + r * (scaled - a * r * r * inner)).astype(BF)
    V.t2()
    for h in range(0, HEADS, 2):
        pair = att[:, h * 128:(h + 2) * 128].T.astype(BF)
        rows_of[:, h * DV:(h + 2) * DV] = jnp.concatenate([pair[:128], pair[128:]], axis=1)
    out[...] = (a + jnp.dot(rows_of[...], wall[:, 1408:2944], preferred_element_type=F32)).astype(BF)
    K.t2()
    V.t3()
    K.t3()
    wgrad[:, 128:320] = V.t4()[:, 0:192]
    wgrad[:, 0:128] = K.t4()


def per_device(act, gain, wq, wk, wv, wo, cot):
    vm = pl.BlockSpec(memory_space=pltpu.VMEM)
    V, DMA = pltpu.VMEM, pltpu.SemaphoreType.DMA
    def slab(rows, cols):
        return [V((16, rows, 128), BF), V((4, 3, rows, 128), BF), V((4, rows, 128), BF), V((2, rows // 2, 128), BF),
                V((2, rows // 2, 128), BF), V((2, rows, 128), BF), V((4, 4, 2, SHARD, cols), BF), V((4, 4, SHARD, cols), BF),
                V((4, 4, SHARD, cols), BF), V((15, SHARD, cols), BF), V((SHARD, cols), BF), V((3, SHARD, cols), BF),
                V((SHARD, cols), BF), V((3, SHARD, cols), BF), DMA((40, 2))]

    scratch = [
        V((1536, COLS), BF), V((16, 320, 128), BF), V((128, 1536), BF), V((128, 1), F32), V((1024, 128), BF), V((1024, 192), BF),
        V((2048, 192), BF), V((2048, 1024), BF), V((192, 2048), BF), V((192, 1024), F32), V((1, 1024), F32), V((1, 1024), F32),
        V((128, 1024), F32), V((128, 1536), BF), V((128, 1536), F32),
        DMA((6,)), DMA((120,)), DMA((2, 6)), DMA((30,)), DMA((30,)),
    ] + slab(128, 128) + slab(192, 256)
    o, i, w = pl.pallas_call(
        body,
        out_shape=(jax.ShapeDtypeStruct((128, 1536), BF), jax.ShapeDtypeStruct((128, 1536), BF),
                   jax.ShapeDtypeStruct((SHARD, 320), F32)),
        in_specs=[vm] * 7, out_specs=(vm,) * 3, scratch_shapes=scratch,
        compiler_params=pltpu.CompilerParams(collective_id=0, has_side_effects=True, vmem_limit_bytes=58 * 2**20),
        name="layer",
    )(act[0], gain, wq, wk, wv, wo, cot[0])
    return o[None], i[None], w


def solution(mesh):
    rows = P("dp", "seq", None)
    split = P("dp", None)
    return jax.shard_map(per_device, mesh=mesh, in_specs=(rows, P(), split, split, split, split, rows),
                         out_specs=(rows, rows, split), check_vma=False)
```

time: 142 us -> 118 us (0.83)
  the two profiles are of different devices: /device:TPU:16 before, /device:TPU:32 now
where the time goes in v2:
time: 118 us
  Pallas kernels  114 us (97%)
  local copies, waits for them, and re-layouts  3.38 us (3%)
    pallas_call x1, Pallas kernels, per_device(): pl.pallas_call(body, out_shape=(jax.ShapeDtypeStruct((128, 1536), BF), ja...  114 us
    unnamed x7, local copies, waits for them, and re-layouts  3.38 us

profile of v2, /device:TPU:32, one launch (start us, length us, event | category | flops | bytes accessed | tf_op | source)
XLA Modules:
  0.0 117.7 jit_solution(12105092621442274168)
XLA Ops:
  0.6 113.7 %layer.1 = (bf16[128,1536]{1,0:T(8,128)(2,1)}, bf16[128,1536]{1,0:T(8,128)(2,1)}, f32[48,320]{1,0:T(8,128)}) custom-call(bf16[128,1536]{1,0:T(8,128)(2,1)} %bitcast.4, f32[1536]{0:T(1024)} %gain.1, bf16[48,1024]{1,0:T(8,128)(2,1)} %wq.1, bf16[48,128]{1,0:T(8,128)(2,1)} %wk.1, bf16[48,192]{1,0:T(8,128)(2,1)} %wv.1, bf16[48,1536]{1,0:T(8,128)(2,1)} %wo.1, ...), custom_call_target="tpu_custom_call" | custom-call | tf_op jit(solution)/shard_map/layer/pallas_call | solution.py:518
  114.3 0.0 copy-start
  114.3 1.8 %copy.13 = bf16[1,128,1536]{2,1,0:T(8,128)(2,1)} copy(bf16[1,128,1536]{2,1,0:T(8,128)(2,1)} %bitcast.7) | data formatting | bytes 786432
  116.1 0.0 copy-done
  116.1 0.0 copy-start.1
  116.1 0.7 copy.14
  116.9 0.2 copy-done.1
  117.1 0.6 copy.15
Async XLA Ops:
  114.3 1.8 %copy-start = (bf16[128,1536]{1,0:T(8,128)(2,1)S(1)}, bf16[128,1536]{1,0:T(8,128)(2,1)}, u32[]{:S(2)}) copy-start(bf16[128,1536]{1,0:T(8,128)(2,1)} %get-tuple-element.7) | copy-start | bytes 1179652
  116.1 0.9 copy-start.1

commit v3 on v2

--- a/solution.py
+++ b/solution.py
@@ -140,10 +140,10 @@
     return ((0, rows, 0, lo), (0, rows, lo, cols - lo))
 
 
-PIECES = ((0, 128, "xz"), (128, 256, "zx"), (384, 384, "xz"), (768, 640, "zx"), (1408, 512, "xz"), (1920, 1024, "zx"))
+PIECES = ((0, 128, "xz"), (128, 256, "zx"), (384, 512, "zx"), (896, 512, "zx"), (1408, 512, "xz"), (1920, 1024, "zx"))
 PLANE = [(dx, 0, dz) for dx in (0, 1, -1, 2) for dz in (0, 1, -1, 2)][1:]
 PEERS = [(2, 0, -2), (1, 0, -2), (-1, 0, -2), (0, 0, -2)] + PLANE + [
-    (0, 1, 0), (0, -1, 0), (0, 2, 0), (0, 0, 4), (0, 0, -4), (0, 0, 8), (0, 0, 0, 1)]
+    (0, 1, 0), (0, -1, 0), (0, 2, 0), (0, 0, 4), (0, 0, -4), (0, 0, 0, 1)]
 
 
 def nt(a, b):
@@ -231,12 +231,12 @@
             self.got(2, 1, 5)
             self.row(2, 1)
 
-        def s6():
-            for kz, half in ((0, 0), (0, 1), (3, 0), (1, 1), (3, 1), (1, 0), (2, 0), (2, 1)):
-                for dy in (1, 3, 2):
-                    self.across(kz, half, dy).wait_recv()
-
-        return [s0, s1, s2, s3, s4, s5, s6]
+        return [s0, s1, s2, s3, s4, s5]
+
+    def settle(self, kz):
+        for half in (0, 1):
+            for dy in (1, 3, 2):
+                self.across(kz, half, dy).wait_recv()
 
     def drain(self):
         for slot in range(30):
@@ -244,20 +244,26 @@
             remote(ref, ref, self.sends.at[slot], self.recvs.at[slot], dev(0, 1)).wait_send()
 
 
-def gather_phase(act, gain, wq, wk, wv, wo, cot, wall, kvp, normed, rs, q, sends, recvs, twins, ksend, krecv):
+def gather_phase(inputs, act, cot, wvs, isem, gain, wall, kvp, normed, rs, q, sends, recvs, twins, ksend, krecv, far, softmax):
     barrier = hello()
     x, y, z, c = spot()
     mine = pl.ds(pl.multiple_of(((x * 4 + lax.rem(z, 4)) * 2 + c) * SHARD, 16), SHARD)
-    wall[mine, 0:128] = wk[...]
+    targets = (act, wall.at[mine, 384:1408], wall.at[mine, 0:128], wvs, wall.at[mine, 1408:2944], cot)
+    loads = [pltpu.make_async_copy(a, b, isem.at[i]) for i, (a, b) in enumerate(zip(inputs, targets))]
+    for i in (0, 2, 3, 1, 4, 5):
+        loads[i].start()
+    loads[3].wait()
     wall[mine, 256:384] = jnp.zeros((SHARD, 128), BF)
-    wall[mine, 128:320] = wv[...]
-    wall[mine, 384:1408] = wq[...]
-    wall[mine, 1408:2944] = wo[...]
+    wall[mine, 128:320] = wvs[...]
+    loads[0].wait()
     wide = act[...].astype(F32)
     r = lax.rsqrt(jnp.mean(wide * wide, axis=-1, keepdims=True) + 1e-6)
     rs[...] = r
     normed[...] = (wide * r * gain[...][None, :]).astype(BF)
+    for i in (2, 1, 4, 5):
+        loads[i].wait()
     pl.semaphore_wait(barrier, len(PEERS))
+    pl.semaphore_signal(far, inc=1, device_id=dev(0, 0, -4), device_id_type=MESH)
 
     def row(order):
         def of(ka, kb):
@@ -289,21 +295,40 @@
     win = Window(kvp, ksend, krecv)
     ks = win.steps()
     ks[0]()
-    do(bulk, 1); do(bulk, 2); do(bulk, 3); do(bulk, 4); do(bulk, 5)
+    first, later = bulk[:2], bulk[2:]
+    do(first, 1); do(first, 2)
+    do(later, 1); do(later, 2)
     ks[1](); ks[2]()
-    do(bulk, 6); do(bulk, 7)
+    for i in (3, 4, 5, 6, 7, 8, 9):
+        do(first, i)
     ks[3](); ks[4]()
-    do(bulk, 8); do(bulk, 9); do(bulk, 10)
+    for i in (3, 4, 5):
+        do(later, i)
     ks[5]()
-    do(bulk, 11); do(bulk, 12); do(bulk, 13); do(bulk, 14); do(bulk, 15)
+    for i in (10, 11, 12):
+        do(first, i)
+    for i in (6, 7, 8, 9):
+        do(later, i)
+    for i in (13, 14, 15):
+        do(first, i)
     parts[2].settle(); parts[3].settle()
     qs = (jnp.dot(normed[...], wall[:, 384:1408], preferred_element_type=F32) * HQ ** -0.5).astype(BF)
     for h in range(HEADS):
         q[pl.ds(h * 128, 128), :] = qs[:, h * HQ:(h + 1) * HQ]
-    ks[6]()
+    win.settle(0)
+    softmax(0)
+    for i in (10, 11, 12):
+        do(later, i)
+    for kz in (3, 1, 2):
+        win.settle(kz)
+        softmax(kz)
+    for i in (13, 14, 15):
+        do(later, i)
+
+    for p in parts[4:]:
+        p.settle()
 
     def finish():
-        parts[4].settle(); parts[5].settle()
         for p in parts:
             p.drain()
         win.drain()
@@ -314,27 +339,30 @@
     return kvp[pl.ds(first, n), 0:128, :].reshape(n * 128, 128)
 
 
-def softmax_phase(q, kvp, v, e, vt, att, inv):
-    v[:, 0:128] = kvp[:, 128:256, :].reshape(2048, 128)
-    v[:, 128:192] = unpack(kvp[:, 256:320, :]).reshape(2048, 64)
-    vt[...] = v[...].T
-    wide = 512
-
-    @pl.loop(0, 1024 // wide)
-    def _(i):
-        at = pl.ds(pl.multiple_of(i * wide, wide), wide)
-        s = nt(keys_of(kvp, 0, 16), q[at, :])
-        p = jnp.exp(s - jnp.max(s, axis=0, keepdims=True))
-        r = 1.0 / jnp.sum(p, axis=0, keepdims=True)
-        pb = p.astype(BF)
-        e[:, at] = pb
-        att[:, at] = jnp.dot(vt[...], pb, preferred_element_type=F32) * r
-        inv[:, at] = r
+def softmax_group(kz, first, q, kvp, v, e, att_of, top, mass):
+    rows = pl.ds(pl.multiple_of(first * 128, 512), 512)
+    v[rows, 0:128] = kvp[pl.ds(first, 4), 128:256, :].reshape(512, 128)
+    v[rows, 128:192] = unpack(kvp[pl.ds(first, 4), 256:320, :]).reshape(512, 64)
+    s = nt(keys_of(kvp, first, 4), q[...])
+    m = jnp.max(s, axis=0, keepdims=True)
+    p = jnp.exp(s - m)
+    top[kz:kz + 1, :] = m
+    mass[kz:kz + 1, :] = jnp.sum(p, axis=0, keepdims=True)
+    pb = p.astype(BF)
+    e[rows, :] = pb
+    att_of[kz] = jnp.dot(v[rows, :].T, pb, preferred_element_type=F32)
+
+
+def softmax_join(att_of, top, mass, att, inv):
+    part = jnp.exp(top[...] - jnp.max(top[...], axis=0, keepdims=True))
+    scale = part / jnp.sum(part * mass[...], axis=0, keepdims=True)
+    inv[...] = scale
+    att[...] = sum(att_of[k] * scale[k:k + 1, :] for k in range(4))
 
 
 def value_terms(first, g, e, inv, part):
     rows = pl.ds(pl.multiple_of(first * 128, 512), 512)
-    p = (e[rows, :].astype(F32) * inv[...]).astype(BF)
+    p = (e[rows, :].astype(F32) * inv).astype(BF)
     dv = jnp.dot(p, g[...], preferred_element_type=F32).astype(BF).reshape(4, 128, 192)
     part[pl.ds(first, 4), 0:128, :] = dv[:, :, 0:128]
     part[pl.ds(first, 4), 128:192, :] = pack(dv[:, :, 128:192])
@@ -343,7 +371,7 @@
 def key_terms(first, q, g, kvp, v, e, inv, centre, part, dqt, start):
     rows = pl.ds(pl.multiple_of(first * 128, 512), 512)
     dp = nt(v[rows, :], g[...])
-    ds = (e[rows, :].astype(F32) * inv[...] * (dp - centre[...])).astype(BF)
+    ds = (e[rows, :].astype(F32) * inv * (dp - centre[...])).astype(BF)
     part[pl.ds(first, 4)] = jnp.dot(ds, q[...], preferred_element_type=F32).astype(BF).reshape(4, 128, 128)
     term = tn(keys_of(kvp, first, 4), ds)
     if start:
@@ -359,27 +387,46 @@
 
 
 class Total:
-    def __init__(self, part, ybuf, zs, mid, fbuf, zbuf, wg, cbuf, xs, xbuf, ps, pbuf, hs, hbuf, sems):
-        self.part, self.ybuf, self.zs, self.mid, self.fbuf, self.zbuf = part, ybuf, zs, mid, fbuf, zbuf
+    def __init__(self, part, yfar, ymid, ynear, zs, mid, fbuf, zbuf, wg, cbuf, xs, xbuf, ps, pbuf, hs, hbuf, sems):
+        self.part, self.yfar, self.ymid, self.ynear = part, yfar, ymid, ynear
+        self.zs, self.mid, self.fbuf, self.zbuf = zs, mid, fbuf, zbuf
         self.wg, self.cbuf, self.xs, self.xbuf, self.ps, self.pbuf = wg, cbuf, xs, xbuf, ps, pbuf
         self.hs, self.hbuf, self.sems = hs, hbuf, sems
         self.rows = part.shape[1]
         self.x, self.y, self.z, self.c = spot()
         self.zh, self.zl = lax.div(self.z, 4), lax.rem(self.z, 4)
-        self.yc, self.zc = {}, []
+        self.yf, self.yc, self.zc = {}, {}, []
 
     def group(self, k):
         return lax.rem(self.zh + k, 4) * 4
 
+    def block(self, k, d):
+        return self.part.at[self.group(k) + lax.rem(self.y + d, 4)]
+
     def y_out(self, k):
-        self.yc[k] = [post(self.part.at[self.group(k) + lax.rem(self.y + dy, 4)], self.ybuf.at[k, dy - 1],
-                           self.sems.at[k * 3 + dy - 1], dev(0, dy)) for dy in (1, 3, 2)]
+        half = self.rows // 2
+        low, high = pl.ds(0, half), pl.ds(half, half)
+        sem = [self.sems.at[40 + 6 * k + i] for i in range(6)]
+        self.yf[k] = [post(self.block(k, 2).at[low], self.yfar.at[k, 0], sem[0], dev(0, 1)),
+                      post(self.block(k, 2).at[high], self.yfar.at[k, 1], sem[1], dev(0, -1))]
+        self.yc[k] = [post(self.block(k, 1).at[high], self.ynear.at[k, 0, high], sem[2], dev(0, 1)),
+                      post(self.block(k, 3).at[low], self.ynear.at[k, 1, low], sem[3], dev(0, -1))]
+
+    def y_mid(self, k):
+        half = self.rows // 2
+        for way in (0, 1):
+            rows = pl.ds(half * way, half)
+            self.yf[k][way].wait()
+            own = self.part[self.group(k) + lax.rem(self.y + (3 if way else 1), 4), rows].astype(F32)
+            self.ymid[k, way] = (own + self.yfar[k, way].astype(F32)).astype(BF)
+            self.yc[k].append(post(self.ymid.at[k, way], self.ynear.at[k, way, rows], self.sems.at[44 + 6 * k + way],
+                                   dev(0, -1 if way else 1)))
 
     def y_in(self, k):
         for cp in self.yc[k]:
             cp.wait()
         f = lambda t: t.astype(F32)
-        self.zs[k] = (f(self.part[self.group(k) + self.y]) + f(self.ybuf[k, 0]) + f(self.ybuf[k, 1]) + f(self.ybuf[k, 2])).astype(BF)
+        self.zs[k] = (f(self.part[self.group(k) + self.y]) + f(self.ynear[k, 0]) + f(self.ynear[k, 1])).astype(BF)
         half = self.rows // 2
         low, high = pl.ds(0, half), pl.ds(half, half)
         if k == 2:
@@ -445,84 +492,116 @@
     return total
 
 
-def body(act, gain, wq, wk, wv, wo, cot, out, ingrad, wgrad,
-         wall, kvp, normed, rs, q, g, v, e, vt, att, inv, centre, dqt, rows_of, ng,
-         sends, recvs, twins, ksend, krecv, *slabs):
-    finish = gather_phase(act, gain, wq, wk, wv, wo, cot, wall, kvp, normed, rs, q, sends, recvs, twins, ksend, krecv)
-    softmax_phase(q, kvp, v, e, vt, att, inv)
-    finish()
+def body(act_in, gain, wq, wk, wv, wo, cot_in, out, ingrad, wgrad,
+         act, cot, wvs, isem, wall, kvp, normed, rs, q, g, v, e, att_of, top, mass, att, inv, centre, dqt, rows_of, ng,
+         sends, recvs, twins, ksend, krecv, far, *slabs):
+    half = len(slabs) // 2
+    K, V = Total(*slabs[:half]), Total(*slabs[half:])
+    finish = gather_phase((act_in, wq, wk, wv, wo, cot_in), act, cot, wvs, isem, gain, wall, kvp, normed, rs, q, sends, recvs, twins,
+                 ksend, krecv, far, lambda kz: softmax_group(kz, K.group(kz), q, kvp, v, e, att_of, top, mass))
     for h in range(HEADS):
         g[pl.ds(h * 128, 128), :] = nt(cot[...], wall[pl.ds(h * DV, DV), 1408:2944]).astype(BF)
-    half = len(slabs) // 2
-    K, V = Total(*slabs[:half]), Total(*slabs[half:])
+    softmax_join(att_of, top, mass, att, inv)
 
     for k in (2, 1, 3, 0):
-        value_terms(V.group(k), g, e, inv, V.part)
+        value_terms(V.group(k), g, e, inv[k:k + 1, :], V.part)
         V.y_out(k)
     centre[...] = jnp.sum(att[...] * g[...].astype(F32).T, axis=0, keepdims=True)
-    for k in (2, 1, 3, 0):
-        key_terms(K.group(k), q, g, kvp, v, e, inv, centre, K.part, dqt, k == 2)
+
+    def keys(k):
+        key_terms(K.group(k), q, g, kvp, v, e, inv[k:k + 1, :], centre, K.part, dqt, k == 2)
         K.y_out(k)
-        if k != 0:
-            V.y_in(k)
+
+    keys(2)
+    V.y_mid(2)
+    V.y_mid(1)
+    keys(1)
+    V.y_mid(3)
+    V.y_mid(0)
+    V.y_in(2)
+    keys(3)
+    V.y_in(1)
+    V.y_in(3)
+    K.y_mid(2)
+    keys(0)
+    K.y_mid(1)
     for h in range(HEADS):
         rows_of[:, h * HQ:(h + 1) * HQ] = (dqt[:, h * 128:(h + 1) * 128].T * HQ ** -0.5).astype(BF)
-    ng[...] = nt(rows_of[:, 0:1024], wall[:, 384:1408])
+    K.y_in(2)
+    K.y_mid(3)
+    K.y_mid(0)
     V.z_mid(0)
     V.z_mid(1)
+    ng[...] = nt(rows_of[:, 0:1024], wall[:, 384:1408])
     V.y_in(0)
-    K.y_in(2)
     K.y_in(1)
     K.y_in(3)
+    K.z_mid(0)
+    K.z_mid(1)
+    K.y_in(0)
+    for h in range(0, HEADS, 2):
+        pair = att[:, h * 128:(h + 2) * 128].T.astype(BF)
+        rows_of[:, h * DV:(h + 2) * DV] = jnp.concatenate([pair[:128], pair[128:]], axis=1)
+    a, r = act[...].astype(F32), rs[...]
+    out[...] = (a + jnp.dot(rows_of[...], wall[:, 1408:2944], preferred_element_type=F32)).astype(BF)
     vsum = V.z_in()
     vgrad = jnp.concatenate([vsum[0:128], unpack(vsum[128:192])], axis=1)
     V.t0(normed, jnp.concatenate([vgrad, jnp.zeros((128, 64), BF)], axis=1))
-    K.z_mid(0)
-    K.z_mid(1)
     V.t1()
-    K.y_in(0)
     kgrad = K.z_in()
     K.t0(normed, kgrad)
     scaled = (ng[...] + nt(jnp.concatenate([kgrad, vgrad], axis=1), wall[:, 0:320])) * gain[...][None, :]
     K.t1()
-    a, r = act[...].astype(F32), rs[...]
     inner = jnp.mean(scaled * a, axis=-1, keepdims=True)
     ingrad[...] = (cot[...].astype(F32) + r * (scaled - a * r * r * inner)).astype(BF)
+    pl.semaphore_wait(far, 1)
     V.t2()
-    for h in range(0, HEADS, 2):
-        pair = att[:, h * 128:(h + 2) * 128].T.astype(BF)
-        rows_of[:, h * DV:(h + 2) * DV] = jnp.concatenate([pair[:128], pair[128:]], axis=1)
-    out[...] = (a + jnp.dot(rows_of[...], wall[:, 1408:2944], preferred_element_type=F32)).astype(BF)
     K.t2()
     V.t3()
     K.t3()
+    finish()
     wgrad[:, 128:320] = V.t4()[:, 0:192]
     wgrad[:, 0:128] = K.t4()
 
 
+def hand_over(a, b, c, to_a, to_b, to_c):
+    to_a[...] = a[...]
+    to_b[...] = b[...]
+    to_c[...] = c[...]
+
+
 def per_device(act, gain, wq, wk, wv, wo, cot):
-    vm = pl.BlockSpec(memory_space=pltpu.VMEM)
+    vm, hbm = pl.BlockSpec(memory_space=pltpu.VMEM), pl.BlockSpec(memory_space=pl.ANY)
     V, DMA = pltpu.VMEM, pltpu.SemaphoreType.DMA
     def slab(rows, cols):
-        return [V((16, rows, 128), BF), V((4, 3, rows, 128), BF), V((4, rows, 128), BF), V((2, rows // 2, 128), BF),
+        return [V((16, rows, 128), BF), V((4, 2, rows // 2, 128), BF), V((4, 2, rows // 2, 128), BF),
+                V((4, 2, rows, 128), BF), V((4, rows, 128), BF), V((2, rows // 2, 128), BF),
                 V((2, rows // 2, 128), BF), V((2, rows, 128), BF), V((4, 4, 2, SHARD, cols), BF), V((4, 4, SHARD, cols), BF),
                 V((4, 4, SHARD, cols), BF), V((15, SHARD, cols), BF), V((SHARD, cols), BF), V((3, SHARD, cols), BF),
-                V((SHARD, cols), BF), V((3, SHARD, cols), BF), DMA((40, 2))]
+                V((SHARD, cols), BF), V((3, SHARD, cols), BF), DMA((64, 2))]
 
     scratch = [
+        V((128, 1536), BF), V((128, 1536), BF), V((SHARD, DV), BF), DMA((6,)),
         V((1536, COLS), BF), V((16, 320, 128), BF), V((128, 1536), BF), V((128, 1), F32), V((1024, 128), BF), V((1024, 192), BF),
-        V((2048, 192), BF), V((2048, 1024), BF), V((192, 2048), BF), V((192, 1024), F32), V((1, 1024), F32), V((1, 1024), F32),
+        V((2048, 192), BF), V((2048, 1024), BF), V((4, 192, 1024), F32), V((4, 1024), F32), V((4, 1024), F32),
+        V((192, 1024), F32), V((4, 1024), F32), V((1, 1024), F32),
         V((128, 1024), F32), V((128, 1536), BF), V((128, 1536), F32),
-        DMA((6,)), DMA((120,)), DMA((2, 6)), DMA((30,)), DMA((30,)),
+        DMA((6,)), DMA((120,)), DMA((2, 6)), DMA((30,)), DMA((30,)), pltpu.SemaphoreType.REGULAR,
     ] + slab(128, 128) + slab(192, 256)
     o, i, w = pl.pallas_call(
         body,
         out_shape=(jax.ShapeDtypeStruct((128, 1536), BF), jax.ShapeDtypeStruct((128, 1536), BF),
                    jax.ShapeDtypeStruct((SHARD, 320), F32)),
-        in_specs=[vm] * 7, out_specs=(vm,) * 3, scratch_shapes=scratch,
+        in_specs=[hbm, vm, hbm, hbm, hbm, hbm, hbm], out_specs=(vm,) * 3, scratch_shapes=scratch,
         compiler_params=pltpu.CompilerParams(collective_id=0, has_side_effects=True, vmem_limit_bytes=58 * 2**20),
         name="layer",
     )(act[0], gain, wq, wk, wv, wo, cot[0])
+    o, i, w = pl.pallas_call(
+        hand_over,
+        out_shape=(jax.ShapeDtypeStruct((128, 1536), BF), jax.ShapeDtypeStruct((128, 1536), BF),
+                   jax.ShapeDtypeStruct((SHARD, 320), F32)),
+        in_specs=[vm] * 3, out_specs=(vm,) * 3, name="hand_over",
+    )(o, i, w)
     return o[None], i[None], w
 
 

time: 118 us -> 115 us (0.975)
  the two profiles are of different devices: /device:TPU:32 before, /device:TPU:6 now
where the time goes in v3:
time: 115 us
  Pallas kernels  114 us (99%)
    pallas_call x1, Pallas kernels, per_device(): pl.pallas_call(body, out_shape=(jax.ShapeDtypeStruct((128, 1536), BF), ja...  112 us

profile of v3, /device:TPU:6, one launch (start us, length us, event | category | flops | bytes accessed | tf_op | source)
XLA Modules:
  0.0 114.7 jit_solution(5295359105086147144)
XLA Ops:
  0.6 112.0 %layer.1 = (bf16[128,1536]{1,0:T(8,128)(2,1)}, bf16[128,1536]{1,0:T(8,128)(2,1)}, f32[48,320]{1,0:T(8,128)}) custom-call(bf16[128,1536]{1,0:T(8,128)(2,1)} %bitcast.4, f32[1536]{0:T(1024)} %gain.1, bf16[48,1024]{1,0:T(8,128)(2,1)} %wq.1, bf16[48,128]{1,0:T(8,128)(2,1)} %wk.1, bf16[48,192]{1,0:T(8,128)(2,1)} %wv.1, bf16[48,1536]{1,0:T(8,128)(2,1)} %wo.1, ...), custom_call_target="tpu_custom_call" | custom-call | tf_op jit(solution)/shard_map/layer/pallas_call | solution.py:591
  112.7 2.0 %hand_over.1 = (bf16[128,1536]{1,0:T(8,128)(2,1)}, bf16[128,1536]{1,0:T(8,128)(2,1)}, f32[48,320]{1,0:T(8,128)}) custom-call(bf16[128,1536]{1,0:T(8,128)(2,1)} %get-tuple-element.9.a, bf16[128,1536]{1,0:T(8,128)(2,1)} %get-tuple-element.10.b, f32[48,320]{1,0:T(8,128)} %get-tuple-element.11.c), custom_call_target="tpu_custom_call" | custom-call | tf_op jit(solution)/shard_map/hand_over/pallas_call | solution.py:599
